TPU v7x, 128 devices: a whole 4x4x4 slice. The times are simulated.
128 devices in a mesh: pb: 8 (over y_lo, x), row: 16 (over z, y_hi, core).
Axes of the slice: x: 4, y: 4 (y_hi: 2, y_lo: 2; y = y_hi * 2 + y_lo), z: 4, core: 2. Of those that a mesh axis runs over, the one named last changes fastest.
Arguments:
- probe_picture_embedding: bfloat16 [16384, 1280], P(('pb', 'row')), may hold values from -8 to 8, as said below
- query_caption_features: bfloat16 [16384, 1024], P(('pb', 'row')), may hold values from -8 to 8, as said below
- ref_image: bfloat16 [32768, 1280], P(('pb', 'row')), may hold values from -8 to 8, as said below
- ref_text: bfloat16 [32768, 1024], P(('pb', 'row')), may hold values from -8 to 8, as said below
- image_head: bfloat16 [1280, 768], replicated, may hold values from -0.15625 to 0.15625
- text_head: bfloat16 [1024, 768], replicated, may hold values from -0.1875 to 0.1875
Outputs:
- pointwise_dependence: float32 [16384], P(('pb', 'row'))
Inputs may be any that keep to these rules, and one draw needn't show every extreme that they name: `probe_picture_embedding`: image features of pairs of one concept lie near a common centre; the caption follows the image's concept in most pairs. `query_caption_features`: text features of pairs of one concept lie near a common centre. `ref_image`: drawn by the same law as the query image features. `ref_text`: drawn by the same law as the query text features.
All inputs are finite; a program needn't handle non-finite values.
Results may differ from a plain program's by a relative error of at most 0.0003.
Values may be sent and summed in bfloat16 or wider, within the bound.
A program may use at most 128 MiB of HBM per device.

v0:
```python
import jax
import jax.numpy as jnp
from jax import lax
from jax.sharding import PartitionSpec as P

epsilon = 1e-05
smoothing_divisor = 0.1


def unit(values):
    width = values.shape[-1]
    scale = lax.rsqrt(jnp.mean(values * values, axis=-1, keepdims=True) + epsilon)
    return values * scale * width ** (-0.5)


def embed(image, text, image_head, text_head):
    emb_image = unit(jnp.dot(image, image_head, preferred_element_type=jnp.float32)).astype(
        jnp.bfloat16
    )
    emb_text = unit(jnp.dot(text, text_head, preferred_element_type=jnp.float32)).astype(
        jnp.bfloat16
    )
    return jnp.concatenate([emb_image, emb_text], axis=1)


def block_sums(queries, reference_pairs):
    width = queries.shape[1] // 2
    visual_similarity_table = jnp.dot(
        queries[:, :width], reference_pairs[:, :width].T, preferred_element_type=jnp.float32
    )
    wording_similarity_table = jnp.dot(
        queries[:, width:], reference_pairs[:, width:].T, preferred_element_type=jnp.float32
    )
    visual_affinity_entries = jnp.exp((visual_similarity_table - 1.0) / smoothing_divisor)
    wording_affinity_entries = jnp.exp((wording_similarity_table - 1.0) / smoothing_divisor)
    return jnp.stack(
        [
            jnp.sum(visual_affinity_entries, axis=1),
            jnp.sum(wording_affinity_entries, axis=1),
            jnp.sum(visual_affinity_entries * wording_affinity_entries, axis=1),
        ],
        axis=0,
    )


def evaluate_sample_dependence(sums, count):
    return jnp.log(sums[2] / count) - jnp.log(sums[0] / count) - jnp.log(sums[1] / count)


def local(
    probe_picture_embedding, query_caption_features, ref_image, ref_text, image_head, text_head
):
    gathered_image, gathered_text = (
        lax.all_gather(probe_picture_embedding, "row", axis=0, tiled=True),
        lax.all_gather(query_caption_features, "row", axis=0, tiled=True),
    )
    queries = embed(gathered_image, gathered_text, image_head, text_head)
    pool_image, pool_text = (
        lax.all_gather(ref_image, "pb", axis=0, tiled=True),
        lax.all_gather(ref_text, "pb", axis=0, tiled=True),
    )
    reference_pairs = embed(pool_image, pool_text, image_head, text_head)
    total = queries.shape[0]
    block = 512
    blocks = queries.reshape(total // block, block, queries.shape[1])
    sums = lax.map(lambda piece: block_sums(piece, reference_pairs), blocks)
    sums = jnp.transpose(sums, (1, 0, 2)).reshape(3, total)
    mine = lax.psum_scatter(sums, "row", scatter_dimension=1, tiled=True)
    count = reference_pairs.shape[0] * lax.axis_size("row")
    return evaluate_sample_dependence(mine, count)


def solution(mesh):
    placed = (
        P(("pb", "row"), None),
        P(("pb", "row"), None),
        P(("pb", "row"), None),
        P(("pb", "row"), None),
        P(),
        P(),
    )
    return jax.shard_map(
        local, mesh=mesh, in_specs=placed, out_specs=P(("pb", "row")), check_vma=False
    )
```

profile of v0, /device:TPU:1, one launch (start us, length us, event | category | flops | bytes accessed | tf_op | source)
XLA Modules:
  0.0 377.5 jit_solution(890806688712509922)
XLA Ops:
  6.5 0.7 all-gather.11.cloned.1.call-update
  9.4 55.4 %all-gather.11.cloned.1.call-done = bf16[2048,1024]{1,0:T(8,128)(2,1)} async-done(((bf16[256,1024]{1,0:T(8,128)(2,1)}), bf16[2048,1024]{1,0:T(8,128)(2,1)}) %all-gather.11.cloned.1.call-update) | async-done | bytes 4194320 | tf_op jit(solution)/shard_map/all_gather | solution.py:60
  64.8 5.9 %multiply_reduce_fusion.1 = (f32[2048]{0:T(1024)S(1)}, f32[2048,768]{0,1:T(8,128)S(1)}) fusion(bf16[2048,1024]{1,0:T(8,128)(2,1)} %all-gather.11.cloned.1.call-done, bf16[1024,768]{1,0:T(8,128)(2,1)} %param.13), kind=kOutput, calls=%fused_computation.14 | convolution fusion | flops 3224369152 | bytes 12066816 | tf_op jit(solution)/shard_map/dot_general | solution.py:20
  70.7 2.5 multiply_convert_fusion
  73.3 4.7 %copy.12 = bf16[2048,768]{1,0:T(8,128)(2,1)} copy(bf16[2048,768]{0,1:T(8,128)(2,1)} %multiply_convert_fusion) | data formatting | bytes 6291456 | tf_op jit(solution)/shard_map/while | solution.py:66
  78.0 44.0 %all-gather.7.cloned.1.call-done = bf16[2048,1024]{1,0:T(8,128)(2,1)} async-done(((bf16[128,1024]{1,0:T(8,128)(2,1)}), bf16[2048,1024]{1,0:T(8,128)(2,1)}) %all-gather.7.cloned.1.call-update) | async-done | bytes 4194320 | tf_op jit(solution)/shard_map/all_gather | solution.py:55
  122.0 8.8 %multiply_reduce_fusion.3 = (f32[2048]{0:T(1024)S(1)}, f32[2048,768]{0,1:T(8,128)}) fusion(bf16[2048,1024]{1,0:T(8,128)(2,1)} %all-gather.7.cloned.1.call-done, bf16[1024,768]{1,0:T(8,128)(2,1)} %param.13), kind=kOutput, calls=%fused_computation.18 | convolution fusion | flops 3224369152 | bytes 12066816 | tf_op jit(solution)/shard_map/dot_general | solution.py:20
  130.8 52.5 %all-gather.9.cloned.1.call-done = bf16[2048,1280]{1,0:T(8,128)(2,1)} async-done(((bf16[256,1280]{1,0:T(8,128)(2,1)}), bf16[2048,1280]{1,0:T(8,128)(2,1)}) %all-gather.9.cloned.1.call-update) | async-done | bytes 5242896 | tf_op jit(solution)/shard_map/all_gather | solution.py:59
  183.3 6.4 %multiply_reduce_fusion.2 = (f32[2048]{0:T(1024)S(1)}, f32[2048,768]{0,1:T(8,128)S(1)}) fusion(bf16[2048,1280]{1,0:T(8,128)(2,1)} %all-gather.9.cloned.1.call-done, bf16[1280,768]{1,0:T(8,128)(2,1)S(1)} %copy-done), kind=kOutput, calls=%fused_computation.16 | convolution fusion | flops 4029675520 | bytes 13508608 | tf_op jit(solution)/shard_map/dot_general | solution.py:17
  189.8 2.6 multiply_convert_fusion.1
  192.4 4.7 %copy.11 = bf16[2048,768]{1,0:T(8,128)(2,1)} copy(bf16[2048,768]{0,1:T(8,128)(2,1)} %multiply_convert_fusion.1) | data formatting | bytes 6291456 | tf_op jit(solution)/shard_map/while | solution.py:66
  197.0 47.8 %all-gather.5.cloned.1.call-done = bf16[2048,1280]{1,0:T(8,128)(2,1)} async-done(((bf16[128,1280]{1,0:T(8,128)(2,1)}), bf16[2048,1280]{1,0:T(8,128)(2,1)}) %all-gather.5.cloned.1.call-update) | async-done | bytes 5242896 | tf_op jit(solution)/shard_map/all_gather | solution.py:54
  244.9 8.7 %multiply_reduce_fusion.4 = (f32[2048]{0:T(1024)S(1)}, f32[2048,768]{0,1:T(8,128)}) fusion(bf16[2048,1280]{1,0:T(8,128)(2,1)} %all-gather.5.cloned.1.call-done, bf16[1280,768]{1,0:T(8,128)(2,1)S(1)} %copy-done), kind=kOutput, calls=%fused_computation.20 | convolution fusion | flops 4029675520 | bytes 13508608 | tf_op jit(solution)/shard_map/dot_general | solution.py:17
  253.6 6.5 %multiply_convert_fusion.2 = (bf16[2048,768]{0,1:T(8,128)(2,1)S(1)}, bf16[2048,768]{0,1:T(8,128)(2,1)S(1)}) fusion(f32[2048,768]{0,1:T(8,128)} %get-tuple-element.114, f32[2048]{0:T(1024)S(1)} %add_rsqrt_fusion.2, f32[2048,768]{0,1:T(8,128)} %get-tuple-element.116, f32[2048]{0:T(1024)S(1)} %add_rsqrt_fusion.3), kind=kLoop, calls=%fused_computation.17 | loop fusion | flops 9437184 | bytes 18890752 | tf_op jit(solution)/shard_map/convert_element_type | solution.py:20
  260.0 3.8 %pad_maximum_fusion = bf16[2048,1536]{0,1:T(8,128)(2,1)} fusion(bf16[2048,768]{0,1:T(8,128)(2,1)S(1)} %get-tuple-element.121, bf16[2048,768]{0,1:T(8,128)(2,1)S(1)} %get-tuple-element.122), kind=kLoop, calls=%fused_computation.12 | loop fusion | flops 12582912 | bytes 12582912 | tf_op jit(solution)/shard_map/concatenate | solution.py:23
  263.8 8.7 %copy.13 = bf16[2048,1536]{1,0:T(8,128)(2,1)} copy(bf16[2048,1536]{0,1:T(8,128)(2,1)} %pad_maximum_fusion) | data formatting | bytes 12582912 | tf_op jit(solution)/shard_map/while | solution.py:66
  272.5 32.7 %while.13 = (s32[]{:T(128)}, f32[4,3,512]{2,1,0:T(4,128)S(1)}, bf16[4,512,1536]{2,1,0:T(8,128)(2,1)}, bf16[2048,768]{1,0:T(8,128)(2,1)}, bf16[2048,768]{1,0:T(8,128)(2,1)}, /*index=5*/s32[]{:T(128)}) while((s32[]{:T(128)}, f32[4,3,512]{2,1,0:T(4,128)S(1)}, bf16[4,512,1536]{2,1,0:T(8,128)(2,1)}, bf16[2048,768]{1,0:T(8,128)(2,1)}, ...), condition=%wide.region_8.9_spmd, body=%wide.region_4.8_spmd.sunk | while | flops 3229615616 | bytes 32002152 | solution.py:66
  272.5 1.5 dynamic-slice_bitcast_fusion.2
  274.0 3.9 %fusion.27 = f32[512,2048]{1,0:T(8,128)S(1)} fusion(bf16[2048,768]{1,0:T(8,128)(2,1)} %get-tuple-element.176, bf16[512,1536]{1,0:T(8,128)(2,1)S(1)} %dynamic-slice_bitcast_fusion.2), kind=kOutput, calls=%fused_computation.6.clone.1 | convolution fusion | flops 1610612736 | bytes 8126464 | tf_op jit(solution)/shard_map/while/body/eval_jaxpr/dot_general | solution.py:31
  277.9 2.7 fusion.28
  280.7 1.5 dynamic-slice_bitcast_fusion.2
  282.2 3.9 %fusion.27 = f32[512,2048]{1,0:T(8,128)S(1)} fusion(bf16[2048,768]{1,0:T(8,128)(2,1)} %get-tuple-element.176, bf16[512,1536]{1,0:T(8,128)(2,1)S(1)} %dynamic-slice_bitcast_fusion.2), kind=kOutput, calls=%fused_computation.6.clone.1 | convolution fusion | flops 1610612736 | bytes 8126464 | tf_op jit(solution)/shard_map/while/body/eval_jaxpr/dot_general | solution.py:31
  286.1 2.7 fusion.28
  288.8 1.5 dynamic-slice_bitcast_fusion.2
  290.4 3.9 %fusion.27 = f32[512,2048]{1,0:T(8,128)S(1)} fusion(bf16[2048,768]{1,0:T(8,128)(2,1)} %get-tuple-element.176, bf16[512,1536]{1,0:T(8,128)(2,1)S(1)} %dynamic-slice_bitcast_fusion.2), kind=kOutput, calls=%fused_computation.6.clone.1 | convolution fusion | flops 1610612736 | bytes 8126464 | tf_op jit(solution)/shard_map/while/body/eval_jaxpr/dot_general | solution.py:31
  294.2 2.7 fusion.28
  297.0 1.5 dynamic-slice_bitcast_fusion.2
  298.6 3.9 %fusion.27 = f32[512,2048]{1,0:T(8,128)S(1)} fusion(bf16[2048,768]{1,0:T(8,128)(2,1)} %get-tuple-element.176, bf16[512,1536]{1,0:T(8,128)(2,1)S(1)} %dynamic-slice_bitcast_fusion.2), kind=kOutput, calls=%fused_computation.6.clone.1 | convolution fusion | flops 1610612736 | bytes 8126464 | tf_op jit(solution)/shard_map/while/body/eval_jaxpr/dot_general | solution.py:31
  302.4 2.7 fusion.28
  305.2 1.3 copy.14
  306.6 62.6 %reduce-scatter.4.cloned.1.call-done = f32[128,3]{1,0:T(8,128)} async-done(((f32[2048,3]{1,0:T(8,128)}), f32[128,3]{1,0:T(8,128)}) %reduce-scatter.4.cloned.1.call-update) | async-done | bytes 1552
  369.2 1.0 fusion.7
  (34 shorter events, 3.0 us)
Async XLA Ops:
  6.5 176.8 %copy-start = (bf16[1280,768]{1,0:T(8,128)(2,1)S(1)}, bf16[1280,768]{1,0:T(8,128)(2,1)}, u32[]{:S(2)}) copy-start(bf16[1280,768]{1,0:T(8,128)(2,1)} %param.12) | copy-start | bytes 5898244
  6.5 58.3 %all-gather.11.cloned.1.call-start = ((), (), s32[]{:S(2)}) async-start(), calls=%async_computation.4 | async-start | bytes 4718592 | tf_op jit(solution)/shard_map/all_gather | solution.py:60
  7.3 114.7 %all-gather.7.cloned.1.call-start = ((), (), s32[]{:S(2)}) async-start(), calls=%async_computation.2 | async-start | bytes 4456448 | tf_op jit(solution)/shard_map/all_gather | solution.py:55
  8.0 175.3 %all-gather.9.cloned.1.call-start = ((), (), s32[]{:S(2)}) async-start(), calls=%async_computation.3 | async-start | bytes 5898240 | tf_op jit(solution)/shard_map/all_gather | solution.py:59
  8.7 236.1 %all-gather.5.cloned.1.call-start = ((), (), s32[]{:S(2)}) async-start(), calls=%async_computation.1 | async-start | bytes 5570560 | tf_op jit(solution)/shard_map/all_gather | solution.py:54
  9.3 359.9 %reduce-scatter.4.cloned.1.call-start = ((), (), s32[]{:S(2)}) async-start(), calls=%async_computation.5 | async-start | bytes 1114112
  274.0 3.9 %copy-start.2 = (bf16[2048,768]{1,0:T(8,128)(2,1)S(1)}, bf16[2048,768]{1,0:T(8,128)(2,1)}, u32[]{:S(2)}) copy-start(bf16[2048,768]{1,0:T(8,128)(2,1)} %get-tuple-element.175) | copy-start | bytes 9437188 | tf_op jit(solution)/shard_map/while
  282.2 3.9 %copy-start.2 = (bf16[2048,768]{1,0:T(8,128)(2,1)S(1)}, bf16[2048,768]{1,0:T(8,128)(2,1)}, u32[]{:S(2)}) copy-start(bf16[2048,768]{1,0:T(8,128)(2,1)} %get-tuple-element.175) | copy-start | bytes 9437188 | tf_op jit(solution)/shard_map/while
  290.4 3.9 %copy-start.2 = (bf16[2048,768]{1,0:T(8,128)(2,1)S(1)}, bf16[2048,768]{1,0:T(8,128)(2,1)}, u32[]{:S(2)}) copy-start(bf16[2048,768]{1,0:T(8,128)(2,1)} %get-tuple-element.175) | copy-start | bytes 9437188 | tf_op jit(solution)/shard_map/while
  298.5 3.9 %copy-start.2 = (bf16[2048,768]{1,0:T(8,128)(2,1)S(1)}, bf16[2048,768]{1,0:T(8,128)(2,1)}, u32[]{:S(2)}) copy-start(bf16[2048,768]{1,0:T(8,128)(2,1)} %get-tuple-element.175) | copy-start | bytes 9437188 | tf_op jit(solution)/shard_map/while
  305.2 65.8 %copy-start.1 = (bf16[1280,768]{1,0:T(8,128)(2,1)S(1)}, bf16[1280,768]{1,0:T(8,128)(2,1)}, u32[]{:S(2)}) copy-start(bf16[1280,768]{1,0:T(8,128)(2,1)} %param.12) | copy-start | bytes 5898244
Sparse Core Ops, SparseCore 0:
  9.0 55.7 all-gather.10
  67.3 54.6 all-gather.6
  123.6 59.6 all-gather.8
  185.7 59.1 all-gather.4
  306.7 62.4 reduce-scatter.3
where the time goes:
time: 379 us; the launch traced here: 378 us
  waiting for transfers between devices  265 us (70%)
  matrix products  56.2 us (15%)
  local copies, waits for them, and re-layouts  26.7 us (7%)
  other arithmetic  16.1 us (4%)
  between operations  13.2 us (3%)
    unnamed x6, waiting for transfers between devices  65.2 us
    all_gather x1, waiting for transfers between devices, local(): lax.all_gather(ref_text, 'pb', axis=0, tiled=True)  55.4 us
    all_gather x1, waiting for transfers between devices, local(): lax.all_gather(ref_image, 'pb', axis=0, tiled=True)  52.5 us
    all_gather x1, waiting for transfers between devices, local(): lax.all_gather(probe_picture_embedding, 'row', axis=0, tiled=True)  47.8 us
    all_gather x1, waiting for transfers between devices, local(): lax.all_gather(query_caption_features, 'row', axis=0, tiled=True)  44 us
    while x3, local copies, waits for them, and re-layouts, local(): sums = lax.map(lambda piece: block_sums(piece, reference_pairs), blocks)  18.1 us
    dot_general x4, matrix products, block_sums(): jnp.dot(queries[:, width:], reference_pairs[:, width:].T, preferred_eleme...  15.4 us
    dot_general x2, matrix products, embed(): jnp.dot(image, image_head, preferred_element_type=jnp.float32)  15.1 us
  transfers between devices with their start and end apart: 5, of which 5 were waited for; matrix products, arithmetic and copies ran while one was open for 9% of the time, Pallas kernels for 0%

commit v1 on v0

v1 whole, which is shorter than its diff:
```python
import functools

import jax
import jax.numpy as jnp
from jax import lax
from jax.experimental import pallas as pl
from jax.experimental.pallas import tpu as pltpu
from jax.sharding import PartitionSpec as P

MESH = pl.DeviceIdType.MESH
EPS = 1e-05
RATE = 10.0 * 1.4426950408889634
E = 768
ROWS_Q = 128
ROWS_R = 256
HALF = 64
N = 4
NT = (((1,), (1,)), ((), ()))

GROUPS = (
    (("A", 0, 0), ("B", 0, 0), ("A", 2, 0), ("B", 0, 2)),
    (("A", -1, 0), ("B", 0, -1), ("A", 1, 0), ("B", 0, 1)),
    (("A", 0, -1), ("B", -1, 0), ("A", 0, 1), ("B", 1, 0)),
    (("A", -1, -1), ("B", -1, -1), ("A", -1, 1), ("B", 1, -1)),
    (("A", 1, -1), ("B", -1, 1), ("A", 1, 1), ("B", 1, 1)),
    (("A", 2, -1), ("B", -1, 2), ("A", 2, 1), ("B", 1, 2)),
    (("A", 0, 2), ("B", 2, 0), ("A", -1, 2), ("B", 2, -1)),
    (("A", 1, 2), ("B", 2, 1), ("A", 2, 2), ("B", 2, 2)),
)
PLACE = {half: i for i, half in enumerate(h for g in GROUPS for h in g)}
SOURCES = tuple((dy, dz) for dy in (0, 1, -1, 2) for dz in (0, 1, -1, 2))
PLANE_DIRS = ((1, 0), (-1, 0), (0, 1), (0, -1))
DEPTH = 3


def wrap(d):
    return (d + 1) % N - 1


def plane_items(direction):
    sy, sz = direction
    if sy:
        h = 0 if sy > 0 else 1
        return (
            ("A", 0, 0, None),
            ("B", 0, 0, None),
            ("A", -sy, 0, h),
            ("B", 0, -1, None),
            ("B", 0, 1, None),
            ("B", -sy, 0, h),
            ("B", 0, 2, None),
            ("B", -sy, -1, h),
            ("B", -sy, 1, h),
            ("B", -sy, 2, h),
        )
    h = 0 if sz > 0 else 1
    return (
        ("B", 0, 0, None),
        ("A", 0, 0, None),
        ("B", 0, -sz, h),
        ("A", -1, 0, None),
        ("A", 1, 0, None),
        ("A", 0, -sz, h),
        ("A", 2, 0, None),
        ("A", -1, -sz, h),
        ("A", 1, -sz, h),
        ("A", 2, -sz, h),
    )


def query_rows(half, dy, dz, part):
    start = PLACE[(half, wrap(dy), wrap(dz))] * HALF
    if part is None:
        return start, HALF
    return start + part * (HALF // 2), HALF // 2


def device_at(x, y, z, c):
    return ((y % 2) * N + x, z * 4 + (y // 2) * 2 + c)


def unit(values):
    scale = lax.rsqrt(jnp.mean(values * values, axis=-1, keepdims=True) + EPS)
    return values * scale * E ** (-0.5)


def kernel(
    qi_hbm, qt_hbm, ri_hbm, rt_hbm, hi_hbm, ht_hbm, out_ref,
    xi, xt, hi, ht, queries, refs, acc, give, take,
    load_sem, plane_send, plane_recv, line_send, line_recv, pair_send, pair_recv, sum_send, sum_recv,
):
    pb, row = lax.axis_index("pb"), lax.axis_index("row")
    x, y = pb % N, (row // 2) % 2 * 2 + pb // N
    z, c = row // 4, row % 2

    def plane(dy, dz):
        return device_at(x, (y + dy + N) % N, (z + dz + N) % N, c)

    def line(dx):
        return device_at((x + dx + N) % N, y, z, c)

    pair = device_at(x, y, z, 1 - c)

    loads = []
    for i, (src, dst) in enumerate(
        (
            (qi_hbm, xi.at[pl.ds(0, ROWS_Q)]),
            (ri_hbm, xi.at[pl.ds(ROWS_Q, ROWS_R)]),
            (hi_hbm, hi),
            (qt_hbm, xt.at[pl.ds(0, ROWS_Q)]),
            (rt_hbm, xt.at[pl.ds(ROWS_Q, ROWS_R)]),
            (ht_hbm, ht),
        )
    ):
        copy = pltpu.make_async_copy(src, dst, load_sem.at[i])
        copy.start()
        loads.append(copy)

    barrier = pltpu.get_barrier_semaphore()
    greeted = [plane(dy, dz) for dy, dz in SOURCES[1:]] + [line(1), line(-1), pair]
    for device in greeted:
        pl.semaphore_signal(barrier, inc=1, device_id=device, device_id_type=MESH)

    acc[...] = jnp.zeros_like(acc)

    def project(features, head, columns):
        made = unit(jnp.dot(features[...], head[...], preferred_element_type=jnp.float32))
        made = made.astype(jnp.bfloat16)
        queries[0:ROWS_Q, columns] = made[:ROWS_Q]
        refs[0:ROWS_R, columns] = made[ROWS_Q:]

    for copy in loads[:3]:
        copy.wait()
    project(xi, hi, slice(0, E))
    for copy in loads[3:]:
        copy.wait()
    project(xt, ht, slice(E, 2 * E))

    pl.semaphore_wait(barrier, len(greeted))

    plane_copies = []
    for k, direction in enumerate(PLANE_DIRS):
        copies = []
        for i, (half, dy, dz, part) in enumerate(plane_items(direction)):
            start, rows = query_rows(half, dy, dz, part)
            there, _ = query_rows(half, dy - direction[0], dz - direction[1], part)
            copies.append(
                pltpu.make_async_remote_copy(
                    src_ref=queries.at[pl.ds(start, rows)],
                    dst_ref=queries.at[pl.ds(there, rows)],
                    send_sem=plane_send.at[k, i],
                    recv_sem=plane_recv.at[k, i],
                    device_id=plane(*direction),
                    device_id_type=MESH,
                )
            )
        plane_copies.append(copies)

    line_copies = []
    for k, dx in enumerate((1, -1)):
        copies = []
        for j in range(6):
            if j < 4:
                start = ((j + 2 * k) % 4) * HALF
            else:
                start = (2 + j - 4) * ROWS_R + k * HALF
            there = (2 + j) * ROWS_R + k * HALF
            copies.append(
                pltpu.make_async_remote_copy(
                    src_ref=refs.at[pl.ds(start, HALF)],
                    dst_ref=refs.at[pl.ds(there, HALF)],
                    send_sem=line_send.at[k, j],
                    recv_sem=line_recv.at[k, j],
                    device_id=line(dx),
                    device_id_type=MESH,
                )
            )
        line_copies.append(copies)
    pair_copies = []
    for j in range(7):
        start = (1 + j) * ROWS_R if j else 0
        there = start + 2 * HALF if j else ROWS_R
        rows = 2 * HALF if j else ROWS_R
        pair_copies.append(
            pltpu.make_async_remote_copy(
                src_ref=refs.at[pl.ds(start, rows)],
                dst_ref=refs.at[pl.ds(there, rows)],
                send_sem=pair_send.at[j],
                recv_sem=pair_recv.at[j],
                device_id=pair,
                device_id_type=MESH,
            )
        )

    def plane_start(i):
        for copies in plane_copies:
            copies[i].start()

    def plane_wait(i):
        for copies in plane_copies:
            copies[i].wait_recv()

    def line_start(j):
        for copies in line_copies:
            copies[j].start()

    def line_wait(j):
        for copies in line_copies:
            copies[j].wait_recv()

    def tile(q0, r0, rows):
        lanes = pl.ds(q0, ROWS_R)
        q = queries[lanes, :]
        r = refs[pl.ds(r0, rows), :]
        gi = lax.dot_general(r[:, :E], q[:, :E], NT, preferred_element_type=jnp.float32)
        gt = lax.dot_general(r[:, E:], q[:, E:], NT, preferred_element_type=jnp.float32)
        ki, kt = jnp.exp2(gi * RATE), jnp.exp2(gt * RATE)
        for k, values in enumerate((ki, kt, ki * kt)):
            acc[k, :, lanes] += jnp.sum(values.reshape(rows // 8, 8, ROWS_R), axis=0)

    def work(g0, groups, b0, blocks):
        rows = blocks * ROWS_R
        pieces = 1 if rows <= 1024 else 2
        rows //= pieces

        def body(i, carry):
            q0 = pl.multiple_of((g0 + i) * ROWS_R, ROWS_R)
            for piece in range(pieces):
                tile(q0, b0 * ROWS_R + piece * rows, rows)
            return carry

        if groups == 1:
            for piece in range(pieces):
                tile(g0 * ROWS_R, b0 * ROWS_R + piece * rows, rows)
        else:
            lax.fori_loop(0, groups, body, 0)

    early = lax.broadcasted_iota(jnp.int32, (1, ROWS_Q), 1) < HALF

    def owned(dy, dz):
        a, b = (PLACE[(h, dy, dz)] // 2 * ROWS_Q for h in "AB")
        rows = []
        for k in range(3):
            sums = acc[k, :, a : a + ROWS_Q]
            if a != b:
                sums = jnp.where(early, sums, acc[k, :, b : b + ROWS_Q])
            rows.append(jnp.sum(sums, axis=0, keepdims=True))
        return jnp.concatenate(rows + [rows[0]] * 5, axis=0)

    sum_copies = {}

    def hand_back(dy, dz):
        i = SOURCES.index((dy, dz)) - 1
        give[i] = owned(dy, dz)
        copy = pltpu.make_async_remote_copy(
            src_ref=give.at[i],
            dst_ref=take.at[i],
            send_sem=sum_send.at[i],
            recv_sem=sum_recv.at[i],
            device_id=plane(dy, dz),
            device_id_type=MESH,
        )
        copy.start()
        sum_copies[i] = copy

    started = 0

    def plane_upto(count):
        nonlocal started
        while started < min(count, 10):
            plane_start(started)
            started += 1

    plane_upto(2)
    line_start(0)
    line_start(1)
    pair_copies[0].start()

    plane_wait(0)
    plane_upto(1 + DEPTH)
    line_wait(0)
    line_start(2)
    pair_copies[1].start()
    pair_copies[0].wait_recv()
    work(1, 1, 0, 2)

    plane_wait(1)
    plane_upto(2 + DEPTH)
    line_wait(1)
    line_start(3)
    pair_copies[2].start()
    work(2, 1, 0, 2)
    pair_copies[1].wait_recv()
    pair_copies[2].wait_recv()
    work(1, 2, 2, 2)

    plane_wait(2)
    plane_upto(3 + DEPTH)
    work(0, 1, 0, 4)
    line_wait(2)
    line_start(4)
    pair_copies[3].start()

    plane_wait(3)
    plane_upto(4 + DEPTH)
    work(3, 1, 0, 4)
    line_wait(3)
    line_start(5)
    pair_copies[4].start()
    pair_copies[3].wait_recv()
    pair_copies[4].wait_recv()
    work(0, 4, 4, 2)

    plane_wait(4)
    plane_upto(5 + DEPTH)
    work(4, 1, 0, 6)

    plane_wait(5)
    plane_upto(6 + DEPTH)
    line_wait(4)
    pair_copies[5].start()
    pair_copies[5].wait_recv()
    work(0, 5, 6, 1)

    plane_wait(6)
    plane_upto(7 + DEPTH)
    line_wait(5)
    pair_copies[6].start()
    work(5, 1, 0, 7)
    pair_copies[6].wait_recv()
    work(0, 6, 7, 1)

    plane_wait(7)
    work(6, 1, 0, 8)
    late = ((1, 2), (2, 1), (2, 2))
    for source in SOURCES[1:]:
        if source not in late:
            hand_back(*source)

    plane_wait(8)
    plane_wait(9)
    work(7, 1, 0, 8)
    for source in late:
        hand_back(*source)

    total = owned(0, 0)
    for i in range(15):
        sum_copies[i].wait_recv()
        total = total + take[i]
    out_ref[...] = total

    for copies in plane_copies + line_copies:
        for copy in copies:
            copy.wait_send()
    for copy in pair_copies:
        copy.wait_send()
    for i in range(15):
        sum_copies[i].wait_send()


def local(query_image, query_text, ref_image, ref_text, image_head, text_head):
    count = ref_image.shape[0] * lax.axis_size("pb") * lax.axis_size("row")
    dma = pltpu.SemaphoreType.DMA
    sums = pl.pallas_call(
        kernel,
        out_shape=jax.ShapeDtypeStruct((8, ROWS_Q), jnp.float32),
        in_specs=[pl.BlockSpec(memory_space=pl.ANY)] * 6,
        out_specs=pl.BlockSpec(memory_space=pltpu.VMEM),
        scratch_shapes=[
            pltpu.VMEM((ROWS_Q + ROWS_R, query_image.shape[1]), jnp.bfloat16),
            pltpu.VMEM((ROWS_Q + ROWS_R, query_text.shape[1]), jnp.bfloat16),
            pltpu.VMEM(image_head.shape, jnp.bfloat16),
            pltpu.VMEM(text_head.shape, jnp.bfloat16),
            pltpu.VMEM((16 * ROWS_Q, 2 * E), jnp.bfloat16),
            pltpu.VMEM((8 * ROWS_R, 2 * E), jnp.bfloat16),
            pltpu.VMEM((3, 8, 16 * ROWS_Q), jnp.float32),
            pltpu.VMEM((15, 8, ROWS_Q), jnp.float32),
            pltpu.VMEM((15, 8, ROWS_Q), jnp.float32),
            dma((6,)),
            dma((4, 10)),
            dma((4, 10)),
            dma((2, 6)),
            dma((2, 6)),
            dma((7,)),
            dma((7,)),
            dma((15,)),
            dma((15,)),
        ],
        compiler_params=pltpu.CompilerParams(
            collective_id=0, has_side_effects=True, vmem_limit_bytes=60 * 2**20
        ),
    )(query_image, query_text, ref_image, ref_text, image_head, text_head)
    return jnp.log(sums[2]) - jnp.log(sums[0]) - jnp.log(sums[1]) + jnp.log(jnp.float32(count))


def solution(mesh):
    split = P(("pb", "row"), None)
    return jax.shard_map(
        local,
        mesh=mesh,
        in_specs=(split, split, split, split, P(), P()),
        out_specs=P(("pb", "row")),
        check_vma=False,
    )
```

time: 379 us -> 54.7 us (0.14)
  waiting for transfers between devices: 265 us -> 0 us
  matrix products: 56.2 us -> 0 us
  Pallas kernels: 0 us -> 53.3 us
  local copies, waits for them, and re-layouts: 26.7 us -> 0 us
  other arithmetic: 16.1 us -> 1.32 us
  between operations: 13.2 us -> 0.01 us
    all_gather x4 -> x0, waiting for transfers between devices: 200 us -> none  [the longest x1 55.4 us: local(): lax.all_gather(ref_text, 'pb', axis=0, tiled=True)]
    unnamed x6 -> x0, waiting for transfers between devices: 65.2 us -> none
    dot_general x12 -> x0, matrix products: 56.2 us -> none  [the longest x4 15.4 us: block_sums(): jnp.dot(queries[:, width:], reference_pairs[:, width:].T, preferred_eleme...]
    pallas_call x0 -> x1, Pallas kernels: none -> 53.3 us  [local(): pl.pallas_call(kernel, out_shape=jax.ShapeDtypeStruct((8, ROWS_Q), jnp.fl...]
    while x11 -> x0, local copies, waits for them, and re-layouts: 18.1 us -> none  [the longest x3 18.1 us: local(): sums = lax.map(lambda piece: block_sums(piece, reference_pairs), blocks)]
    convert_element_type x3 -> x0, other arithmetic: 11.6 us -> none  [the longest x2 9.03 us: embed(): unit(jnp.dot(text, text_head, preferred_element_type=jnp.float32))]
    squeeze x4 -> x0, local copies, waits for them, and re-layouts: 6.05 us -> none  [local(): sums = lax.map(lambda piece: block_sums(piece, reference_pairs), blocks)]
  transfers between devices with their start and end apart: 5 -> 0, of which waited for: 5 -> 0; matrix products, arithmetic and copies ran while one was open for 9% -> 0% of each run, Pallas kernels for 0% -> 0%
where the time goes in v1:
time: 54.7 us; the launch traced here: 54.6 us
  Pallas kernels  53.3 us (97%)
  other arithmetic  1.32 us (2%)
    pallas_call x1, Pallas kernels, local(): pl.pallas_call(kernel, out_shape=jax.ShapeDtypeStruct((8, ROWS_Q), jnp.fl...  53.3 us
    add x1, other arithmetic, local(): jnp.log(sums[2]) - jnp.log(sums[0]) - jnp.log(sums[1])  1.32 us

profile of v1, /device:TPU:1, one launch (start us, length us, event | category | flops | bytes accessed | tf_op | source)
XLA Modules:
  0.0 54.6 jit_solution(1419255989370144398)
XLA Ops:
  0.0 53.3 %shard_map.64 = f32[8,128]{1,0:T(8,128)} custom-call(bf16[128,1280]{1,0:T(8,128)(2,1)} %qi_hbm.1, bf16[128,1024]{1,0:T(8,128)(2,1)} %qt_hbm.1, bf16[256,1280]{1,0:T(8,128)(2,1)} %ri_hbm.1, bf16[256,1024]{1,0:T(8,128)(2,1)} %rt_hbm.1, bf16[1280,768]{1,0:T(8,128)(2,1)} %hi_hbm.1, bf16[1024,768]{1,0:T(8,128)(2,1)} %ht_hbm.1), custom_call_target="tpu_custom_call" | custom-call | tf_op jit(solution)/shard_map/pallas_call | solution.py:364
  53.3 1.3 %add_bitcast_fusion = f32[128]{0:T(128)} fusion(f32[8,128]{1,0:T(8,128)} %shard_map.64), kind=kLoop, calls=%fused_computation | loop fusion | flops 384 | bytes 2048 | tf_op jit(solution)/shard_map/add | solution.py:393

commit v2 on v1

--- a/solution.py
+++ b/solution.py
@@ -30,42 +30,39 @@
 PLACE = {half: i for i, half in enumerate(h for g in GROUPS for h in g)}
 SOURCES = tuple((dy, dz) for dy in (0, 1, -1, 2) for dz in (0, 1, -1, 2))
 PLANE_DIRS = ((1, 0), (-1, 0), (0, 1), (0, -1))
-DEPTH = 3
 
 
 def wrap(d):
     return (d + 1) % N - 1
 
 
+BOTH, IMAGE, TEXT = slice(0, 2 * E), slice(0, E), slice(E, 2 * E)
+
+
 def plane_items(direction):
-    sy, sz = direction
-    if sy:
-        h = 0 if sy > 0 else 1
-        return (
-            ("A", 0, 0, None),
-            ("B", 0, 0, None),
-            ("A", -sy, 0, h),
-            ("B", 0, -1, None),
-            ("B", 0, 1, None),
-            ("B", -sy, 0, h),
-            ("B", 0, 2, None),
-            ("B", -sy, -1, h),
-            ("B", -sy, 1, h),
-            ("B", -sy, 2, h),
-        )
-    h = 0 if sz > 0 else 1
-    return (
-        ("B", 0, 0, None),
-        ("A", 0, 0, None),
-        ("B", 0, -sz, h),
-        ("A", -1, 0, None),
-        ("A", 1, 0, None),
-        ("A", 0, -sz, h),
-        ("A", 2, 0, None),
-        ("A", -1, -sz, h),
-        ("A", 1, -sz, h),
-        ("A", 2, -sz, h),
+    s = sum(direction)
+    h = 0 if s > 0 else 1
+    items = (
+        ("A", 0, 0, None, IMAGE),
+        ("A", 0, 0, None, TEXT),
+        ("B", 0, 0, None, BOTH),
+        ("A", -s, 0, h, BOTH),
+        ("B", 0, -1, None, BOTH),
+        ("B", 0, 1, None, BOTH),
+        ("B", -s, 0, h, BOTH),
+        ("B", 0, 2, None, BOTH),
+        ("B", -s, -1, h, BOTH),
+        ("B", -s, 1, h, IMAGE),
+        ("B", -s, 2, h, IMAGE),
+        ("B", -s, 1, h, TEXT),
+        ("B", -s, 2, h, TEXT),
     )
+    if direction[0]:
+        return items
+    return tuple(("AB"["BA".index(half)], dz, dy, part, columns) for half, dy, dz, part, columns in items)
+
+
+UPTO = (3, 5, 6, 7, 8, 9, 10, 12, 13)
 
 
 def query_rows(half, dy, dz, part):
@@ -86,7 +83,7 @@
 
 def kernel(
     qi_hbm, qt_hbm, ri_hbm, rt_hbm, hi_hbm, ht_hbm, out_ref,
-    xi, xt, hi, ht, queries, refs, acc, give, take,
+    qi, qt, ri, rt, hi, ht, queries, refs, acc, kept, give, take,
     load_sem, plane_send, plane_recv, line_send, line_recv, pair_send, pair_recv, sum_send, sum_recv,
 ):
     pb, row = lax.axis_index("pb"), lax.axis_index("row")
@@ -104,12 +101,12 @@
     loads = []
     for i, (src, dst) in enumerate(
         (
-            (qi_hbm, xi.at[pl.ds(0, ROWS_Q)]),
-            (ri_hbm, xi.at[pl.ds(ROWS_Q, ROWS_R)]),
+            (qi_hbm, qi),
             (hi_hbm, hi),
-            (qt_hbm, xt.at[pl.ds(0, ROWS_Q)]),
-            (rt_hbm, xt.at[pl.ds(ROWS_Q, ROWS_R)]),
+            (qt_hbm, qt),
             (ht_hbm, ht),
+            (ri_hbm, ri),
+            (rt_hbm, rt),
         )
     ):
         copy = pltpu.make_async_copy(src, dst, load_sem.at[i])
@@ -117,37 +114,26 @@
         loads.append(copy)
 
     barrier = pltpu.get_barrier_semaphore()
-    greeted = [plane(dy, dz) for dy, dz in SOURCES[1:]] + [line(1), line(-1), pair]
+    greeted = [plane(dy, dz) for dy, dz in PLANE_DIRS] + [line(1), line(-1), pair]
     for device in greeted:
         pl.semaphore_signal(barrier, inc=1, device_id=device, device_id_type=MESH)
 
     acc[...] = jnp.zeros_like(acc)
 
-    def project(features, head, columns):
+    def project(features, head, rows, columns, into):
         made = unit(jnp.dot(features[...], head[...], preferred_element_type=jnp.float32))
-        made = made.astype(jnp.bfloat16)
-        queries[0:ROWS_Q, columns] = made[:ROWS_Q]
-        refs[0:ROWS_R, columns] = made[ROWS_Q:]
-
-    for copy in loads[:3]:
-        copy.wait()
-    project(xi, hi, slice(0, E))
-    for copy in loads[3:]:
-        copy.wait()
-    project(xt, ht, slice(E, 2 * E))
-
-    pl.semaphore_wait(barrier, len(greeted))
+        into[0:rows, columns] = made.astype(jnp.bfloat16)
 
     plane_copies = []
     for k, direction in enumerate(PLANE_DIRS):
         copies = []
-        for i, (half, dy, dz, part) in enumerate(plane_items(direction)):
+        for i, (half, dy, dz, part, columns) in enumerate(plane_items(direction)):
             start, rows = query_rows(half, dy, dz, part)
             there, _ = query_rows(half, dy - direction[0], dz - direction[1], part)
             copies.append(
                 pltpu.make_async_remote_copy(
-                    src_ref=queries.at[pl.ds(start, rows)],
-                    dst_ref=queries.at[pl.ds(there, rows)],
+                    src_ref=queries.at[pl.ds(start, rows), columns],
+                    dst_ref=queries.at[pl.ds(there, rows), columns],
                     send_sem=plane_send.at[k, i],
                     recv_sem=plane_recv.at[k, i],
                     device_id=plane(*direction),
@@ -208,32 +194,31 @@
         for copies in line_copies:
             copies[j].wait_recv()
 
+    def affinity(q0, lanes, r0, rows, columns):
+        gram = lax.dot_general(
+            refs[pl.ds(r0, rows), columns],
+            queries[pl.ds(q0, lanes), columns],
+            NT,
+            preferred_element_type=jnp.float32,
+        )
+        return jnp.exp2(gram * RATE)
+
+    def add(k, q0, lanes, values):
+        acc[k, :, pl.ds(q0, lanes)] += jnp.sum(values.reshape(-1, 8, lanes), axis=0)
+
     def tile(q0, r0, rows):
-        lanes = pl.ds(q0, ROWS_R)
-        q = queries[lanes, :]
-        r = refs[pl.ds(r0, rows), :]
-        gi = lax.dot_general(r[:, :E], q[:, :E], NT, preferred_element_type=jnp.float32)
-        gt = lax.dot_general(r[:, E:], q[:, E:], NT, preferred_element_type=jnp.float32)
-        ki, kt = jnp.exp2(gi * RATE), jnp.exp2(gt * RATE)
+        ki = affinity(q0, ROWS_R, r0, rows, IMAGE)
+        kt = affinity(q0, ROWS_R, r0, rows, TEXT)
         for k, values in enumerate((ki, kt, ki * kt)):
-            acc[k, :, lanes] += jnp.sum(values.reshape(rows // 8, 8, ROWS_R), axis=0)
+            add(k, q0, ROWS_R, values)
 
     def work(g0, groups, b0, blocks):
         rows = blocks * ROWS_R
         pieces = 1 if rows <= 1024 else 2
         rows //= pieces
-
-        def body(i, carry):
-            q0 = pl.multiple_of((g0 + i) * ROWS_R, ROWS_R)
+        for g in range(g0, g0 + groups):
             for piece in range(pieces):
-                tile(q0, b0 * ROWS_R + piece * rows, rows)
-            return carry
-
-        if groups == 1:
-            for piece in range(pieces):
-                tile(g0 * ROWS_R, b0 * ROWS_R + piece * rows, rows)
-        else:
-            lax.fori_loop(0, groups, body, 0)
+                tile(g * ROWS_R, b0 * ROWS_R + piece * rows, rows)
 
     early = lax.broadcasted_iota(jnp.int32, (1, ROWS_Q), 1) < HALF
 
@@ -247,12 +232,8 @@
             rows.append(jnp.sum(sums, axis=0, keepdims=True))
         return jnp.concatenate(rows + [rows[0]] * 5, axis=0)
 
-    sum_copies = {}
-
-    def hand_back(dy, dz):
-        i = SOURCES.index((dy, dz)) - 1
-        give[i] = owned(dy, dz)
-        copy = pltpu.make_async_remote_copy(
+    sum_copies = [
+        pltpu.make_async_remote_copy(
             src_ref=give.at[i],
             dst_ref=take.at[i],
             send_sem=sum_send.at[i],
@@ -260,32 +241,55 @@
             device_id=plane(dy, dz),
             device_id_type=MESH,
         )
-        copy.start()
-        sum_copies[i] = copy
+        for i, (dy, dz) in enumerate(SOURCES[1:])
+    ]
+
+    def hand_back(sources):
+        which = [SOURCES.index(source) - 1 for source in sources]
+        for i, source in zip(which, sources):
+            give[i] = owned(*source)
+        for i in which:
+            sum_copies[i].start()
 
     started = 0
 
     def plane_upto(count):
         nonlocal started
-        while started < min(count, 10):
-            plane_start(started)
-            started += 1
-
-    plane_upto(2)
+        for i in range(started, count):
+            plane_start(i)
+        started = max(started, count)
+
+    def plane_next(i):
+        plane_wait(i)
+        if i < len(UPTO):
+            plane_upto(UPTO[i])
+
+    loads[0].wait()
+    loads[1].wait()
+    project(qi, hi, ROWS_Q, IMAGE, queries)
+    pl.semaphore_wait(barrier, len(greeted))
+    plane_upto(1)
+    loads[2].wait()
+    loads[3].wait()
+    project(qt, ht, ROWS_Q, TEXT, queries)
+    plane_upto(3)
+    loads[4].wait()
+    project(ri, hi, ROWS_R, IMAGE, refs)
+    loads[5].wait()
+    project(rt, ht, ROWS_R, TEXT, refs)
     line_start(0)
     line_start(1)
     pair_copies[0].start()
 
-    plane_wait(0)
-    plane_upto(1 + DEPTH)
+    plane_next(0)
+    plane_next(1)
     line_wait(0)
     line_start(2)
     pair_copies[1].start()
     pair_copies[0].wait_recv()
     work(1, 1, 0, 2)
 
-    plane_wait(1)
-    plane_upto(2 + DEPTH)
+    plane_next(2)
     line_wait(1)
     line_start(3)
     pair_copies[2].start()
@@ -294,15 +298,13 @@
     pair_copies[2].wait_recv()
     work(1, 2, 2, 2)
 
-    plane_wait(2)
-    plane_upto(3 + DEPTH)
+    plane_next(3)
     work(0, 1, 0, 4)
     line_wait(2)
     line_start(4)
     pair_copies[3].start()
 
-    plane_wait(3)
-    plane_upto(4 + DEPTH)
+    plane_next(4)
     work(3, 1, 0, 4)
     line_wait(3)
     line_start(5)
@@ -311,37 +313,41 @@
     pair_copies[4].wait_recv()
     work(0, 4, 4, 2)
 
-    plane_wait(4)
-    plane_upto(5 + DEPTH)
+    plane_next(5)
     work(4, 1, 0, 6)
 
-    plane_wait(5)
-    plane_upto(6 + DEPTH)
+    plane_next(6)
     line_wait(4)
     pair_copies[5].start()
     pair_copies[5].wait_recv()
     work(0, 5, 6, 1)
 
-    plane_wait(6)
-    plane_upto(7 + DEPTH)
+    plane_next(7)
     line_wait(5)
     pair_copies[6].start()
     work(5, 1, 0, 7)
     pair_copies[6].wait_recv()
     work(0, 6, 7, 1)
 
-    plane_wait(7)
+    plane_next(8)
     work(6, 1, 0, 8)
     late = ((1, 2), (2, 1), (2, 2))
-    for source in SOURCES[1:]:
-        if source not in late:
-            hand_back(*source)
-
-    plane_wait(8)
-    plane_wait(9)
-    work(7, 1, 0, 8)
-    for source in late:
-        hand_back(*source)
+    hand_back([source for source in SOURCES[1:] if source not in late])
+
+    last = 7 * ROWS_R
+    plane_next(9)
+    plane_next(10)
+    for piece in range(2):
+        ki = affinity(last, ROWS_R, piece * 1024, 1024, IMAGE)
+        kept[pl.ds(piece * 1024, 1024), :] = ki
+        add(0, last, ROWS_R, ki)
+    plane_next(11)
+    plane_next(12)
+    for piece in range(2):
+        kt = affinity(last, ROWS_R, piece * 1024, 1024, TEXT)
+        add(1, last, ROWS_R, kt)
+        add(2, last, ROWS_R, kt * kept[pl.ds(piece * 1024, 1024), :])
+    hand_back(late)
 
     total = owned(0, 0)
     for i in range(15):
@@ -354,8 +360,8 @@
             copy.wait_send()
     for copy in pair_copies:
         copy.wait_send()
-    for i in range(15):
-        sum_copies[i].wait_send()
+    for copy in sum_copies:
+        copy.wait_send()
 
 
 def local(query_image, query_text, ref_image, ref_text, image_head, text_head):
@@ -367,18 +373,21 @@
         in_specs=[pl.BlockSpec(memory_space=pl.ANY)] * 6,
         out_specs=pl.BlockSpec(memory_space=pltpu.VMEM),
         scratch_shapes=[
-            pltpu.VMEM((ROWS_Q + ROWS_R, query_image.shape[1]), jnp.bfloat16),
-            pltpu.VMEM((ROWS_Q + ROWS_R, query_text.shape[1]), jnp.bfloat16),
+            pltpu.VMEM(query_image.shape, jnp.bfloat16),
+            pltpu.VMEM(query_text.shape, jnp.bfloat16),
+            pltpu.VMEM(ref_image.shape, jnp.bfloat16),
+            pltpu.VMEM(ref_text.shape, jnp.bfloat16),
             pltpu.VMEM(image_head.shape, jnp.bfloat16),
             pltpu.VMEM(text_head.shape, jnp.bfloat16),
             pltpu.VMEM((16 * ROWS_Q, 2 * E), jnp.bfloat16),
             pltpu.VMEM((8 * ROWS_R, 2 * E), jnp.bfloat16),
             pltpu.VMEM((3, 8, 16 * ROWS_Q), jnp.float32),
+            pltpu.VMEM((8 * ROWS_R, ROWS_R), jnp.float32),
             pltpu.VMEM((15, 8, ROWS_Q), jnp.float32),
             pltpu.VMEM((15, 8, ROWS_Q), jnp.float32),
             dma((6,)),
-            dma((4, 10)),
-            dma((4, 10)),
+            dma((4, 13)),
+            dma((4, 13)),
             dma((2, 6)),
             dma((2, 6)),
             dma((7,)),

time: 54.7 us -> 53.4 us (0.976)
  Pallas kernels: 53.3 us -> 51.6 us
    pallas_call x1, Pallas kernels: 53.3 us -> 51.6 us  [local(): pl.pallas_call(kernel, out_shape=jax.ShapeDtypeStruct((8, ROWS_Q), jnp.fl...]
where the time goes in v2:
time: 53.4 us; the launch traced here: 52.9 us
  Pallas kernels  51.6 us (97%)
  other arithmetic  1.32 us (2%)
    pallas_call x1, Pallas kernels, local(): pl.pallas_call(kernel, out_shape=jax.ShapeDtypeStruct((8, ROWS_Q), jnp.fl...  51.6 us
    add x1, other arithmetic, local(): jnp.log(sums[2]) - jnp.log(sums[0]) - jnp.log(sums[1])  1.32 us

profile of v2, /device:TPU:1, one launch (start us, length us, event | category | flops | bytes accessed | tf_op | source)
XLA Modules:
  0.0 52.9 jit_solution(15196039314064699228)
XLA Ops:
  0.0 51.6 %shard_map.64 = f32[8,128]{1,0:T(8,128)} custom-call(bf16[128,1280]{1,0:T(8,128)(2,1)} %qi_hbm.1, bf16[128,1024]{1,0:T(8,128)(2,1)} %qt_hbm.1, bf16[256,1280]{1,0:T(8,128)(2,1)} %ri_hbm.1, bf16[256,1024]{1,0:T(8,128)(2,1)} %rt_hbm.1, bf16[1280,768]{1,0:T(8,128)(2,1)} %hi_hbm.1, bf16[1024,768]{1,0:T(8,128)(2,1)} %ht_hbm.1), custom_call_target="tpu_custom_call" | custom-call | tf_op jit(solution)/shard_map/pallas_call | solution.py:370
  51.6 1.3 %add_bitcast_fusion = f32[128]{0:T(128)} fusion(f32[8,128]{1,0:T(8,128)} %shard_map.64), kind=kLoop, calls=%fused_computation | loop fusion | flops 384 | bytes 2048 | tf_op jit(solution)/shard_map/add | solution.py:402

commit v3 on v2

--- a/solution.py
+++ b/solution.py
@@ -22,10 +22,10 @@
     (("A", -1, 0), ("B", 0, -1), ("A", 1, 0), ("B", 0, 1)),
     (("A", 0, -1), ("B", -1, 0), ("A", 0, 1), ("B", 1, 0)),
     (("A", -1, -1), ("B", -1, -1), ("A", -1, 1), ("B", 1, -1)),
+    (("A", 2, -1), ("B", -1, 2), ("A", 2, 1), ("B", 1, 2)),
     (("A", 1, -1), ("B", -1, 1), ("A", 1, 1), ("B", 1, 1)),
-    (("A", 2, -1), ("B", -1, 2), ("A", 2, 1), ("B", 1, 2)),
-    (("A", 0, 2), ("B", 2, 0), ("A", -1, 2), ("B", 2, -1)),
-    (("A", 1, 2), ("B", 2, 1), ("A", 2, 2), ("B", 2, 2)),
+    (("A", 2, 2), ("B", 2, 2), ("A", -1, 2), ("B", 2, -1)),
+    (("A", 1, 2), ("B", 2, 1), ("A", 0, 2), ("B", 2, 0)),
 )
 PLACE = {half: i for i, half in enumerate(h for g in GROUPS for h in g)}
 SOURCES = tuple((dy, dz) for dy in (0, 1, -1, 2) for dz in (0, 1, -1, 2))
@@ -36,33 +36,30 @@
     return (d + 1) % N - 1
 
 
-BOTH, IMAGE, TEXT = slice(0, 2 * E), slice(0, E), slice(E, 2 * E)
+IMAGE, TEXT = slice(0, E), slice(E, 2 * E)
 
 
 def plane_items(direction):
     s = sum(direction)
     h = 0 if s > 0 else 1
     items = (
-        ("A", 0, 0, None, IMAGE),
-        ("A", 0, 0, None, TEXT),
-        ("B", 0, 0, None, BOTH),
-        ("A", -s, 0, h, BOTH),
-        ("B", 0, -1, None, BOTH),
-        ("B", 0, 1, None, BOTH),
-        ("B", -s, 0, h, BOTH),
-        ("B", 0, 2, None, BOTH),
-        ("B", -s, -1, h, BOTH),
-        ("B", -s, 1, h, IMAGE),
-        ("B", -s, 2, h, IMAGE),
-        ("B", -s, 1, h, TEXT),
-        ("B", -s, 2, h, TEXT),
+        ("A", 0, 0, None),
+        ("B", 0, 0, None),
+        ("A", -s, 0, h),
+        ("B", 0, -1, None),
+        ("B", 0, 2, None),
+        ("B", 0, 1, None),
+        ("B", -s, 2, h),
+        ("B", -s, -1, h),
+        ("B", -s, 1, h),
+        ("B", -s, 0, h),
     )
     if direction[0]:
         return items
-    return tuple(("AB"["BA".index(half)], dz, dy, part, columns) for half, dy, dz, part, columns in items)
-
-
-UPTO = (3, 5, 6, 7, 8, 9, 10, 12, 13)
+    return tuple(("AB"["BA".index(half)], dz, dy, part) for half, dy, dz, part in items)
+
+
+UPTO = (4, 4, 6, 6, 8, 10)
 
 
 def query_rows(half, dy, dz, part):
@@ -83,7 +80,7 @@
 
 def kernel(
     qi_hbm, qt_hbm, ri_hbm, rt_hbm, hi_hbm, ht_hbm, out_ref,
-    qi, qt, ri, rt, hi, ht, queries, refs, acc, kept, give, take,
+    qi, qt, ri, rt, hi, ht, queries, refs, acc, give, take,
     load_sem, plane_send, plane_recv, line_send, line_recv, pair_send, pair_recv, sum_send, sum_recv,
 ):
     pb, row = lax.axis_index("pb"), lax.axis_index("row")
@@ -127,13 +124,13 @@
     plane_copies = []
     for k, direction in enumerate(PLANE_DIRS):
         copies = []
-        for i, (half, dy, dz, part, columns) in enumerate(plane_items(direction)):
+        for i, (half, dy, dz, part) in enumerate(plane_items(direction)):
             start, rows = query_rows(half, dy, dz, part)
             there, _ = query_rows(half, dy - direction[0], dz - direction[1], part)
             copies.append(
                 pltpu.make_async_remote_copy(
-                    src_ref=queries.at[pl.ds(start, rows), columns],
-                    dst_ref=queries.at[pl.ds(there, rows), columns],
+                    src_ref=queries.at[pl.ds(start, rows)],
+                    dst_ref=queries.at[pl.ds(there, rows)],
                     send_sem=plane_send.at[k, i],
                     recv_sem=plane_recv.at[k, i],
                     device_id=plane(*direction),
@@ -206,19 +203,21 @@
     def add(k, q0, lanes, values):
         acc[k, :, pl.ds(q0, lanes)] += jnp.sum(values.reshape(-1, 8, lanes), axis=0)
 
-    def tile(q0, r0, rows):
-        ki = affinity(q0, ROWS_R, r0, rows, IMAGE)
-        kt = affinity(q0, ROWS_R, r0, rows, TEXT)
+    def tile(q0, lanes, r0, rows):
+        ki = affinity(q0, lanes, r0, rows, IMAGE)
+        kt = affinity(q0, lanes, r0, rows, TEXT)
         for k, values in enumerate((ki, kt, ki * kt)):
-            add(k, q0, ROWS_R, values)
-
-    def work(g0, groups, b0, blocks):
+            add(k, q0, lanes, values)
+
+    def work(q0, lanes, b0, blocks):
         rows = blocks * ROWS_R
         pieces = 1 if rows <= 1024 else 2
-        rows //= pieces
+        for piece in range(pieces):
+            tile(q0, lanes, b0 * ROWS_R + piece * (rows // pieces), rows // pieces)
+
+    def work_groups(g0, groups, b0, blocks):
         for g in range(g0, g0 + groups):
-            for piece in range(pieces):
-                tile(g * ROWS_R, b0 * ROWS_R + piece * rows, rows)
+            work(g * ROWS_R, ROWS_R, b0, blocks)
 
     early = lax.broadcasted_iota(jnp.int32, (1, ROWS_Q), 1) < HALF
 
@@ -230,7 +229,7 @@
             if a != b:
                 sums = jnp.where(early, sums, acc[k, :, b : b + ROWS_Q])
             rows.append(jnp.sum(sums, axis=0, keepdims=True))
-        return jnp.concatenate(rows + [rows[0]] * 5, axis=0)
+        return jnp.concatenate(rows + [rows[0]], axis=0)
 
     sum_copies = [
         pltpu.make_async_remote_copy(
@@ -267,86 +266,73 @@
     loads[0].wait()
     loads[1].wait()
     project(qi, hi, ROWS_Q, IMAGE, queries)
-    pl.semaphore_wait(barrier, len(greeted))
-    plane_upto(1)
     loads[2].wait()
     loads[3].wait()
     project(qt, ht, ROWS_Q, TEXT, queries)
-    plane_upto(3)
+    pl.semaphore_wait(barrier, len(greeted))
+    plane_upto(2)
     loads[4].wait()
     project(ri, hi, ROWS_R, IMAGE, refs)
     loads[5].wait()
     project(rt, ht, ROWS_R, TEXT, refs)
+    pair_copies[0].start()
     line_start(0)
     line_start(1)
-    pair_copies[0].start()
+    line_start(2)
+
+    def line_next(j):
+        line_wait(j)
+        if j < 3:
+            line_start(j + 3)
+        pair_copies[j + 1].start()
 
     plane_next(0)
+    pair_copies[0].wait_recv()
+    work_groups(1, 1, 0, 2)
+    line_next(0)
+
     plane_next(1)
-    line_wait(0)
-    line_start(2)
-    pair_copies[1].start()
-    pair_copies[0].wait_recv()
-    work(1, 1, 0, 2)
+    work_groups(2, 1, 0, 2)
+    pair_copies[1].wait_recv()
+    work_groups(1, 2, 2, 1)
+    line_next(1)
 
     plane_next(2)
-    line_wait(1)
-    line_start(3)
-    pair_copies[2].start()
-    work(2, 1, 0, 2)
-    pair_copies[1].wait_recv()
     pair_copies[2].wait_recv()
-    work(1, 2, 2, 2)
+    work_groups(0, 1, 0, 4)
+    work_groups(1, 2, 3, 1)
+    line_next(2)
 
     plane_next(3)
-    work(0, 1, 0, 4)
-    line_wait(2)
-    line_start(4)
-    pair_copies[3].start()
+    pair_copies[3].wait_recv()
+    work_groups(3, 1, 0, 5)
+    work_groups(0, 3, 4, 1)
+    line_next(3)
 
     plane_next(4)
-    work(3, 1, 0, 4)
-    line_wait(3)
-    line_start(5)
-    pair_copies[4].start()
-    pair_copies[3].wait_recv()
     pair_copies[4].wait_recv()
-    work(0, 4, 4, 2)
+    work_groups(4, 1, 0, 6)
+    work_groups(0, 4, 5, 1)
+    line_next(4)
 
     plane_next(5)
-    work(4, 1, 0, 6)
+    pair_copies[5].wait_recv()
+    work_groups(5, 1, 0, 7)
+    work_groups(0, 5, 6, 1)
+
+    line_next(5)
+    pair_copies[6].wait_recv()
+    work_groups(0, 6, 7, 1)
 
     plane_next(6)
-    line_wait(4)
-    pair_copies[5].start()
-    pair_copies[5].wait_recv()
-    work(0, 5, 6, 1)
-
     plane_next(7)
-    line_wait(5)
-    pair_copies[6].start()
-    work(5, 1, 0, 7)
-    pair_copies[6].wait_recv()
-    work(0, 6, 7, 1)
+    work_groups(6, 1, 0, 8)
+    late = ((1, 2), (2, 1), (0, 2), (2, 0))
+    hand_back([source for source in SOURCES[1:] if source not in late])
 
     plane_next(8)
-    work(6, 1, 0, 8)
-    late = ((1, 2), (2, 1), (2, 2))
-    hand_back([source for source in SOURCES[1:] if source not in late])
-
-    last = 7 * ROWS_R
     plane_next(9)
-    plane_next(10)
-    for piece in range(2):
-        ki = affinity(last, ROWS_R, piece * 1024, 1024, IMAGE)
-        kept[pl.ds(piece * 1024, 1024), :] = ki
-        add(0, last, ROWS_R, ki)
-    plane_next(11)
-    plane_next(12)
-    for piece in range(2):
-        kt = affinity(last, ROWS_R, piece * 1024, 1024, TEXT)
-        add(1, last, ROWS_R, kt)
-        add(2, last, ROWS_R, kt * kept[pl.ds(piece * 1024, 1024), :])
+    work_groups(7, 1, 0, 8)
     hand_back(late)
 
     total = owned(0, 0)
@@ -369,8 +355,8 @@
     dma = pltpu.SemaphoreType.DMA
     sums = pl.pallas_call(
         kernel,
-        out_shape=jax.ShapeDtypeStruct((8, ROWS_Q), jnp.float32),
-        in_specs=[pl.BlockSpec(memory_space=pl.ANY)] * 6,
+        out_shape=pltpu.VMEM((4, ROWS_Q), jnp.float32),
+        in_specs=[pl.BlockSpec(memory_space=pltpu.HBM)] * 6,
         out_specs=pl.BlockSpec(memory_space=pltpu.VMEM),
         scratch_shapes=[
             pltpu.VMEM(query_image.shape, jnp.bfloat16),
@@ -382,12 +368,11 @@
             pltpu.VMEM((16 * ROWS_Q, 2 * E), jnp.bfloat16),
             pltpu.VMEM((8 * ROWS_R, 2 * E), jnp.bfloat16),
             pltpu.VMEM((3, 8, 16 * ROWS_Q), jnp.float32),
-            pltpu.VMEM((8 * ROWS_R, ROWS_R), jnp.float32),
-            pltpu.VMEM((15, 8, ROWS_Q), jnp.float32),
-            pltpu.VMEM((15, 8, ROWS_Q), jnp.float32),
+            pltpu.VMEM((15, 4, ROWS_Q), jnp.float32),
+            pltpu.VMEM((15, 4, ROWS_Q), jnp.float32),
             dma((6,)),
-            dma((4, 13)),
-            dma((4, 13)),
+            dma((4, 10)),
+            dma((4, 10)),
             dma((2, 6)),
             dma((2, 6)),
             dma((7,)),
@@ -396,7 +381,7 @@
             dma((15,)),
         ],
         compiler_params=pltpu.CompilerParams(
-            collective_id=0, has_side_effects=True, vmem_limit_bytes=60 * 2**20
+            collective_id=0, has_side_effects=True, vmem_limit_bytes=63 * 2**20
         ),
     )(query_image, query_text, ref_image, ref_text, image_head, text_head)
     return jnp.log(sums[2]) - jnp.log(sums[0]) - jnp.log(sums[1]) + jnp.log(jnp.float32(count))

time: 53.4 us -> 51.4 us (0.963)
  Pallas kernels: 51.6 us -> 50.6 us
  other arithmetic: 1.32 us -> 0.52 us
    pallas_call x1, Pallas kernels: 51.6 us -> 50.6 us  [local(): pl.pallas_call(kernel, out_shape=pltpu.VMEM((4, ROWS_Q), jnp.float32), in...]
    add x1, other arithmetic: 1.32 us -> 0.52 us  [local(): jnp.log(sums[2]) - jnp.log(sums[0]) - jnp.log(sums[1])]
where the time goes in v3:
time: 51.4 us; the launch traced here: 51.1 us
  Pallas kernels  50.6 us (98%)
  other arithmetic  0.52 us (1%)
    pallas_call x1, Pallas kernels, local(): pl.pallas_call(kernel, out_shape=pltpu.VMEM((4, ROWS_Q), jnp.float32), in...  50.6 us

profile of v3, /device:TPU:1, one launch (start us, length us, event | category | flops | bytes accessed | tf_op | source)
XLA Modules:
  0.0 51.1 jit_solution(2268432695335810710)
XLA Ops:
  0.0 50.6 %shard_map.64 = f32[4,128]{1,0:T(4,128)S(1)} custom-call(bf16[128,1280]{1,0:T(8,128)(2,1)} %qi_hbm.1, bf16[128,1024]{1,0:T(8,128)(2,1)} %qt_hbm.1, bf16[256,1280]{1,0:T(8,128)(2,1)} %ri_hbm.1, bf16[256,1024]{1,0:T(8,128)(2,1)} %rt_hbm.1, bf16[1280,768]{1,0:T(8,128)(2,1)} %hi_hbm.1, bf16[1024,768]{1,0:T(8,128)(2,1)} %ht_hbm.1), custom_call_target="tpu_custom_call" | custom-call | tf_op jit(solution)/shard_map/pallas_call | solution.py:356
  50.6 0.5 %add_bitcast_fusion = f32[128]{0:T(128)} fusion(f32[4,128]{1,0:T(4,128)S(1)} %shard_map.64), kind=kLoop, calls=%fused_computation | loop fusion | flops 384 | bytes 2048 | tf_op jit(solution)/shard_map/add | solution.py:387

commit v4 on v3

--- a/solution.py
+++ b/solution.py
@@ -266,19 +266,19 @@
     loads[0].wait()
     loads[1].wait()
     project(qi, hi, ROWS_Q, IMAGE, queries)
+    loads[4].wait()
+    project(ri, hi, ROWS_R, IMAGE, refs)
     loads[2].wait()
     loads[3].wait()
     project(qt, ht, ROWS_Q, TEXT, queries)
+    loads[5].wait()
     pl.semaphore_wait(barrier, len(greeted))
     plane_upto(2)
-    loads[4].wait()
-    project(ri, hi, ROWS_R, IMAGE, refs)
-    loads[5].wait()
     project(rt, ht, ROWS_R, TEXT, refs)
-    pair_copies[0].start()
     line_start(0)
     line_start(1)
     line_start(2)
+    pair_copies[0].start()
 
     def line_next(j):
         line_wait(j)
@@ -320,15 +320,15 @@
     work_groups(5, 1, 0, 7)
     work_groups(0, 5, 6, 1)
 
-    line_next(5)
-    pair_copies[6].wait_recv()
-    work_groups(0, 6, 7, 1)
-
     plane_next(6)
     plane_next(7)
-    work_groups(6, 1, 0, 8)
+    line_next(5)
+    work_groups(6, 1, 0, 7)
+    pair_copies[6].wait_recv()
+    work_groups(0, 7, 7, 1)
     late = ((1, 2), (2, 1), (0, 2), (2, 0))
-    hand_back([source for source in SOURCES[1:] if source not in late])
+    soon = [source for source in SOURCES[1:] if source not in late]
+    hand_back(soon)
 
     plane_next(8)
     plane_next(9)
@@ -336,9 +336,11 @@
     hand_back(late)
 
     total = owned(0, 0)
-    for i in range(15):
-        sum_copies[i].wait_recv()
-        total = total + take[i]
+    for sources in (soon, late):
+        for source in sources:
+            i = SOURCES.index(source) - 1
+            sum_copies[i].wait_recv()
+            total = total + take[i]
     out_ref[...] = total
 
     for copies in plane_copies + line_copies:

time: 51.4 us -> 50.2 us (0.977)
  Pallas kernels: 50.6 us -> 49.5 us
    pallas_call x1, Pallas kernels: 50.6 us -> 49.5 us  [local(): pl.pallas_call(kernel, out_shape=pltpu.VMEM((4, ROWS_Q), jnp.float32), in...]
where the time goes in v4:
time: 50.2 us; the launch traced here: 50.1 us
  Pallas kernels  49.5 us (99%)
  other arithmetic  0.52 us (1%)
    pallas_call x1, Pallas kernels, local(): pl.pallas_call(kernel, out_shape=pltpu.VMEM((4, ROWS_Q), jnp.float32), in...  49.5 us

profile of v4, /device:TPU:1, one launch (start us, length us, event | category | flops | bytes accessed | tf_op | source)
XLA Modules:
  0.0 50.1 jit_solution(9253201428249743416)
XLA Ops:
  0.0 49.5 %shard_map.64 = f32[4,128]{1,0:T(4,128)S(1)} custom-call(bf16[128,1280]{1,0:T(8,128)(2,1)} %qi_hbm.1, bf16[128,1024]{1,0:T(8,128)(2,1)} %qt_hbm.1, bf16[256,1280]{1,0:T(8,128)(2,1)} %ri_hbm.1, bf16[256,1024]{1,0:T(8,128)(2,1)} %rt_hbm.1, bf16[1280,768]{1,0:T(8,128)(2,1)} %hi_hbm.1, bf16[1024,768]{1,0:T(8,128)(2,1)} %ht_hbm.1), custom_call_target="tpu_custom_call" | custom-call | tf_op jit(solution)/shard_map/pallas_call | solution.py:358
  49.5 0.5 %add_bitcast_fusion = f32[128]{0:T(128)} fusion(f32[4,128]{1,0:T(4,128)S(1)} %shard_map.64), kind=kLoop, calls=%fused_computation | loop fusion | flops 384 | bytes 2048 | tf_op jit(solution)/shard_map/add | solution.py:389

commit v5 on v4

--- a/solution.py
+++ b/solution.py
@@ -17,17 +17,26 @@
 N = 4
 NT = (((1,), (1,)), ((), ()))
 
-GROUPS = (
-    (("A", 0, 0), ("B", 0, 0), ("A", 2, 0), ("B", 0, 2)),
-    (("A", -1, 0), ("B", 0, -1), ("A", 1, 0), ("B", 0, 1)),
-    (("A", 0, -1), ("B", -1, 0), ("A", 0, 1), ("B", 1, 0)),
-    (("A", -1, -1), ("B", -1, -1), ("A", -1, 1), ("B", 1, -1)),
-    (("A", 2, -1), ("B", -1, 2), ("A", 2, 1), ("B", 1, 2)),
-    (("A", 1, -1), ("B", -1, 1), ("A", 1, 1), ("B", 1, 1)),
-    (("A", 2, 2), ("B", 2, 2), ("A", -1, 2), ("B", 2, -1)),
-    (("A", 1, 2), ("B", 2, 1), ("A", 0, 2), ("B", 2, 0)),
+COLUMNS = (
+    ((0, 0), (0, 0), (0, 0), (0, 0)),
+    ((2, 0), (2, 0), (0, 2), (0, 2)),
+    ((-1, 0), (-1, 0), (0, -1), (0, -1)),
+    ((1, 0), (1, 0), (0, 1), (0, 1)),
+    ((0, -1), (0, -1), (-1, 0), (-1, 0)),
+    ((0, 1), (0, 1), (1, 0), (1, 0)),
+    ((-1, -1), (-1, -1), (-1, -1), (-1, -1)),
+    ((-1, 1), (-1, 1), (1, -1), (1, -1)),
+    ((2, -1), (2, -1), (-1, 2), (-1, 2)),
+    ((2, 1), (2, 1), (1, 2), (1, 2)),
+    ((1, -1), (1, 1), (-1, 1), (1, 1)),
+    ((1, 2), (1, 2), (2, 1), (2, 1)),
+    ((-1, 2), (-1, 2), (2, -1), (2, -1)),
+    ((2, 2), (2, 2), (2, 2), (2, 2)),
+    ((0, 2), (0, 2), (2, 0), (2, 0)),
+    ((1, 1), (1, -1), (1, 1), (-1, 1)),
 )
-PLACE = {half: i for i, half in enumerate(h for g in GROUPS for h in g)}
+QUARTER = 32
+PLACE = {("AABB"[q], q % 2, *source): 4 * i + q for i, column in enumerate(COLUMNS) for q, source in enumerate(column)}
 SOURCES = tuple((dy, dz) for dy in (0, 1, -1, 2) for dz in (0, 1, -1, 2))
 PLANE_DIRS = ((1, 0), (-1, 0), (0, 1), (0, -1))
 
@@ -46,27 +55,26 @@
         ("A", 0, 0, None),
         ("B", 0, 0, None),
         ("A", -s, 0, h),
+        ("B", 0, 1, h),
         ("B", 0, -1, None),
         ("B", 0, 2, None),
-        ("B", 0, 1, None),
+        ("B", -s, 1, h),
+        ("B", -s, -1, h),
         ("B", -s, 2, h),
-        ("B", -s, -1, h),
-        ("B", -s, 1, h),
         ("B", -s, 0, h),
+        ("B", -2 * s, 1, h),
     )
     if direction[0]:
         return items
     return tuple(("AB"["BA".index(half)], dz, dy, part) for half, dy, dz, part in items)
 
 
-UPTO = (4, 4, 6, 6, 8, 10)
+UPTO = (5, 5, 6, 7, 8, 10, 11)
 
 
 def query_rows(half, dy, dz, part):
-    start = PLACE[(half, wrap(dy), wrap(dz))] * HALF
-    if part is None:
-        return start, HALF
-    return start + part * (HALF // 2), HALF // 2
+    start = PLACE[(half, part or 0, wrap(dy), wrap(dz))] * QUARTER
+    return start, HALF if part is None else QUARTER
 
 
 def device_at(x, y, z, c):
@@ -219,15 +227,16 @@
         for g in range(g0, g0 + groups):
             work(g * ROWS_R, ROWS_R, b0, blocks)
 
-    early = lax.broadcasted_iota(jnp.int32, (1, ROWS_Q), 1) < HALF
+    quarter = lax.broadcasted_iota(jnp.int32, (1, ROWS_Q), 1) // QUARTER
 
     def owned(dy, dz):
-        a, b = (PLACE[(h, dy, dz)] // 2 * ROWS_Q for h in "AB")
+        places = [PLACE[(half, part, dy, dz)] // 4 * ROWS_Q for half in "AB" for part in range(2)]
         rows = []
         for k in range(3):
-            sums = acc[k, :, a : a + ROWS_Q]
-            if a != b:
-                sums = jnp.where(early, sums, acc[k, :, b : b + ROWS_Q])
+            sums = acc[k, :, places[0] : places[0] + ROWS_Q]
+            for q in range(1, 4):
+                if places[q] != places[q - 1]:
+                    sums = jnp.where(quarter < q, sums, acc[k, :, places[q] : places[q] + ROWS_Q])
             rows.append(jnp.sum(sums, axis=0, keepdims=True))
         return jnp.concatenate(rows + [rows[0]], axis=0)
 
@@ -266,18 +275,21 @@
     loads[0].wait()
     loads[1].wait()
     project(qi, hi, ROWS_Q, IMAGE, queries)
-    loads[4].wait()
-    project(ri, hi, ROWS_R, IMAGE, refs)
     loads[2].wait()
     loads[3].wait()
     project(qt, ht, ROWS_Q, TEXT, queries)
-    loads[5].wait()
     pl.semaphore_wait(barrier, len(greeted))
     plane_upto(2)
+    loads[4].wait()
+    project(ri, hi, ROWS_R, IMAGE, refs)
+    loads[5].wait()
     project(rt, ht, ROWS_R, TEXT, refs)
     line_start(0)
     line_start(1)
     line_start(2)
+    late = ((2, 0), (0, 2), (1, 1), (1, -1), (-1, 1))
+    soon = [source for source in SOURCES[1:] if source not in late]
+
     pair_copies[0].start()
 
     def line_next(j):
@@ -304,34 +316,33 @@
     line_next(2)
 
     plane_next(3)
+    plane_next(4)
     pair_copies[3].wait_recv()
     work_groups(3, 1, 0, 5)
     work_groups(0, 3, 4, 1)
     line_next(3)
 
-    plane_next(4)
+    plane_next(5)
     pair_copies[4].wait_recv()
     work_groups(4, 1, 0, 6)
     work_groups(0, 4, 5, 1)
     line_next(4)
 
-    plane_next(5)
+    plane_next(6)
     pair_copies[5].wait_recv()
     work_groups(5, 1, 0, 7)
     work_groups(0, 5, 6, 1)
 
-    plane_next(6)
+    line_next(5)
     plane_next(7)
-    line_next(5)
+    plane_next(8)
     work_groups(6, 1, 0, 7)
     pair_copies[6].wait_recv()
     work_groups(0, 7, 7, 1)
-    late = ((1, 2), (2, 1), (0, 2), (2, 0))
-    soon = [source for source in SOURCES[1:] if source not in late]
     hand_back(soon)
 
-    plane_next(8)
     plane_next(9)
+    plane_next(10)
     work_groups(7, 1, 0, 8)
     hand_back(late)
 
@@ -373,8 +384,8 @@
             pltpu.VMEM((15, 4, ROWS_Q), jnp.float32),
             pltpu.VMEM((15, 4, ROWS_Q), jnp.float32),
             dma((6,)),
-            dma((4, 10)),
-            dma((4, 10)),
+            dma((4, 11)),
+            dma((4, 11)),
             dma((2, 6)),
             dma((2, 6)),
             dma((7,)),

time: 50.2 us -> 50.1 us (level)
  no operation moved by 1% of the time
where the time goes in v5:
time: 50.1 us; the launch traced here: 50 us
  Pallas kernels  49.5 us (99%)
  other arithmetic  0.52 us (1%)
    pallas_call x1, Pallas kernels, local(): pl.pallas_call(kernel, out_shape=pltpu.VMEM((4, ROWS_Q), jnp.float32), in...  49.5 us

profile of v5, /device:TPU:1, one launch (start us, length us, event | category | flops | bytes accessed | tf_op | source)
XLA Modules:
  0.0 50.0 jit_solution(6429468850907380688)
XLA Ops:
  0.0 49.5 %shard_map.64 = f32[4,128]{1,0:T(4,128)S(1)} custom-call(bf16[128,1280]{1,0:T(8,128)(2,1)} %qi_hbm.1, bf16[128,1024]{1,0:T(8,128)(2,1)} %qt_hbm.1, bf16[256,1280]{1,0:T(8,128)(2,1)} %ri_hbm.1, bf16[256,1024]{1,0:T(8,128)(2,1)} %rt_hbm.1, bf16[1280,768]{1,0:T(8,128)(2,1)} %hi_hbm.1, bf16[1024,768]{1,0:T(8,128)(2,1)} %ht_hbm.1), custom_call_target="tpu_custom_call" | custom-call | tf_op jit(solution)/shard_map/pallas_call | solution.py:369
  49.5 0.5 %add_bitcast_fusion = f32[128]{0:T(128)} fusion(f32[4,128]{1,0:T(4,128)S(1)} %shard_map.64), kind=kLoop, calls=%fused_computation | loop fusion | flops 384 | bytes 2048 | tf_op jit(solution)/shard_map/add | solution.py:400

commit v6 on v5

--- a/solution.py
+++ b/solution.py
@@ -103,13 +103,17 @@
 
     pair = device_at(x, y, z, 1 - c)
 
+    def halves(src, dst):
+        rows = src.shape[0] // 2
+        return [(src.at[pl.ds(p * rows, rows)], dst.at[pl.ds(p * rows, rows)]) for p in range(2)]
+
     loads = []
     for i, (src, dst) in enumerate(
         (
             (qi_hbm, qi),
-            (hi_hbm, hi),
+            *halves(hi_hbm, hi),
             (qt_hbm, qt),
-            (ht_hbm, ht),
+            *halves(ht_hbm, ht),
             (ri_hbm, ri),
             (rt_hbm, rt),
         )
@@ -125,8 +129,15 @@
 
     acc[...] = jnp.zeros_like(acc)
 
-    def project(features, head, rows, columns, into):
-        made = unit(jnp.dot(features[...], head[...], preferred_element_type=jnp.float32))
+    def project(features, head, rows, columns, into, needs):
+        depth = head.shape[0] // 2
+        made = 0.0
+        for p in range(2):
+            for n in needs[p]:
+                loads[n].wait()
+            part = slice(p * depth, (p + 1) * depth)
+            made += jnp.dot(features[:, part], head[part, :], preferred_element_type=jnp.float32)
+        made = unit(made)
         into[0:rows, columns] = made.astype(jnp.bfloat16)
 
     plane_copies = []
@@ -272,18 +283,12 @@
         if i < len(UPTO):
             plane_upto(UPTO[i])
 
-    loads[0].wait()
-    loads[1].wait()
-    project(qi, hi, ROWS_Q, IMAGE, queries)
-    loads[2].wait()
-    loads[3].wait()
-    project(qt, ht, ROWS_Q, TEXT, queries)
+    project(qi, hi, ROWS_Q, IMAGE, queries, ((0, 1), (2,)))
+    project(qt, ht, ROWS_Q, TEXT, queries, ((3, 4), (5,)))
     pl.semaphore_wait(barrier, len(greeted))
     plane_upto(2)
-    loads[4].wait()
-    project(ri, hi, ROWS_R, IMAGE, refs)
-    loads[5].wait()
-    project(rt, ht, ROWS_R, TEXT, refs)
+    project(ri, hi, ROWS_R, IMAGE, refs, ((6,), ()))
+    project(rt, ht, ROWS_R, TEXT, refs, ((7,), ()))
     line_start(0)
     line_start(1)
     line_start(2)
@@ -383,7 +388,7 @@
             pltpu.VMEM((3, 8, 16 * ROWS_Q), jnp.float32),
             pltpu.VMEM((15, 4, ROWS_Q), jnp.float32),
             pltpu.VMEM((15, 4, ROWS_Q), jnp.float32),
-            dma((6,)),
+            dma((8,)),
             dma((4, 11)),
             dma((4, 11)),
             dma((2, 6)),

time: 50.1 us -> 50.3 us (level)
  no operation moved by 1% of the time
where the time goes in v6:
time: 50.3 us; the launch traced here: 50.2 us
  Pallas kernels  49.7 us (99%)
  other arithmetic  0.52 us (1%)
    pallas_call x1, Pallas kernels, local(): pl.pallas_call(kernel, out_shape=pltpu.VMEM((4, ROWS_Q), jnp.float32), in...  49.7 us

profile of v6, /device:TPU:1, one launch (start us, length us, event | category | flops | bytes accessed | tf_op | source)
XLA Modules:
  0.0 50.2 jit_solution(5942264820606617165)
XLA Ops:
  0.0 49.7 %shard_map.64 = f32[4,128]{1,0:T(4,128)S(1)} custom-call(bf16[128,1280]{1,0:T(8,128)(2,1)} %qi_hbm.1, bf16[128,1024]{1,0:T(8,128)(2,1)} %qt_hbm.1, bf16[256,1280]{1,0:T(8,128)(2,1)} %ri_hbm.1, bf16[256,1024]{1,0:T(8,128)(2,1)} %rt_hbm.1, bf16[1280,768]{1,0:T(8,128)(2,1)} %hi_hbm.1, bf16[1024,768]{1,0:T(8,128)(2,1)} %ht_hbm.1), custom_call_target="tpu_custom_call" | custom-call | tf_op jit(solution)/shard_map/pallas_call | solution.py:374
  49.7 0.5 %add_bitcast_fusion = f32[128]{0:T(128)} fusion(f32[4,128]{1,0:T(4,128)S(1)} %shard_map.64), kind=kLoop, calls=%fused_computation | loop fusion | flops 384 | bytes 2048 | tf_op jit(solution)/shard_map/add | solution.py:405

commit v7 on v5

--- a/solution.py
+++ b/solution.py
@@ -340,13 +340,13 @@
     pair_copies[6].wait_recv()
     work_groups(0, 7, 7, 1)
     hand_back(soon)
+    total = owned(0, 0)
 
     plane_next(9)
     plane_next(10)
     work_groups(7, 1, 0, 8)
     hand_back(late)
 
-    total = owned(0, 0)
     for sources in (soon, late):
         for source in sources:
             i = SOURCES.index(source) - 1

time: 50.1 us -> 50.1 us (level)
  no operation moved by 1% of the time
where the time goes in v7:
time: 50.1 us; the launch traced here: 50 us
  Pallas kernels  49.5 us (99%)
  other arithmetic  0.52 us (1%)
    pallas_call x1, Pallas kernels, local(): pl.pallas_call(kernel, out_shape=pltpu.VMEM((4, ROWS_Q), jnp.float32), in...  49.5 us

profile of v7, /device:TPU:1, one launch (start us, length us, event | category | flops | bytes accessed | tf_op | source)
XLA Modules:
  0.0 50.0 jit_solution(9463711576272987491)
XLA Ops:
  0.0 49.5 %shard_map.64 = f32[4,128]{1,0:T(4,128)S(1)} custom-call(bf16[128,1280]{1,0:T(8,128)(2,1)} %qi_hbm.1, bf16[128,1024]{1,0:T(8,128)(2,1)} %qt_hbm.1, bf16[256,1280]{1,0:T(8,128)(2,1)} %ri_hbm.1, bf16[256,1024]{1,0:T(8,128)(2,1)} %rt_hbm.1, bf16[1280,768]{1,0:T(8,128)(2,1)} %hi_hbm.1, bf16[1024,768]{1,0:T(8,128)(2,1)} %ht_hbm.1), custom_call_target="tpu_custom_call" | custom-call | tf_op jit(solution)/shard_map/pallas_call | solution.py:369
  49.5 0.5 %add_bitcast_fusion = f32[128]{0:T(128)} fusion(f32[4,128]{1,0:T(4,128)S(1)} %shard_map.64), kind=kLoop, calls=%fused_computation | loop fusion | flops 384 | bytes 2048 | tf_op jit(solution)/shard_map/add | solution.py:400
